TPU v7x, 32 devices: a whole 2x2x4 slice. The times are simulated.
32 devices in a mesh: grp: 2 (over y), blk: 4 (over z), col: 2 (over x), rhs: 2 (over core).
Axes of the slice: x: 2, y: 2, z: 4, core: 2. Of those that a mesh axis runs over, the one named last changes fastest.
Arguments:
- vector: bfloat16 [8192, 256], P(('grp', 'blk'), 'rhs'), parts along dimension 0, may hold values from -24 to 24
- self_term: float32 [8192], P(('grp', 'blk')), parts along dimension 0, may hold values from 1 to 4
- near_blocks: bfloat16 [480, 256, 256], P(('grp', 'blk', 'col')), parts along dimension 0, may hold values from -0.09375 to 0.09375
- near_rows: int32 [480], P(('grp', 'blk', 'col')), parts along dimension 0, may hold values from 0 to 3
- near_source: int32 [480], P(('grp', 'blk', 'col')), parts along dimension 0, may hold values from 0 to 7, as said below
- send_index: int32 [8, 4], P(('grp', 'blk')), parts along dimension 0, may hold values from 0 to 4, as said below
- source_basis: bfloat16 [32, 32, 256], P(('grp', 'blk')), parts along dimension 0, may hold values from -0.375 to 0.375
- target_basis: bfloat16 [32, 32, 256], P(('grp', 'blk')), parts along dimension 0, may hold values from -1 to 1
- couplings: bfloat16 [1024, 32, 32], P(('grp', 'blk', 'col')), parts along dimension 0, may hold values from -0.1875 to 0.1875
- far_rows: int32 [1024], P(('grp', 'blk', 'col')), parts along dimension 0, may hold values from 0 to 3
- far_cols: int32 [1024], P(('grp', 'blk', 'col')), parts along dimension 0, may hold values from 0 to 15
Outputs:
- last_vector: bfloat16 [8192, 256], P(('grp', 'blk', 'col'), 'rhs'), parts along dimension 0
- hessenberg: float32 [18, 256], P('grp', 'rhs'), parts along dimension 0
There are 2 independent parts, one for each index of `grp`. A program takes and returns all parts, laid end to end along the dimension named above; each array names one. Nothing has to cross between parts.
Inputs may be any that keep to these rules, and one draw needn't show every extreme that they name: send_index[s, d] is a cluster of owner s counted within s, or 4 if owner d reads none from s; send_index[d, d] is 4; some owner reads one cluster from every other owner. `near_source`: values at least 4 name an owner s = value - 4 with send_index[s, d] below 4; every cluster that send_index names is used by some near block of its reader.
All inputs are finite; a program needn't handle non-finite values.
Results may differ from a plain program's by a relative error of at most 0.015.
Values may be sent and summed in bfloat16 or wider, within the bound.
A program may use at most 64 MiB of HBM per device.

v0:
```python
import jax
import jax.numpy as jnp
from jax import lax
from jax.sharding import PartitionSpec as P

ITERS = 3


def orthogonalize(work, basis, panels, reduce_small):
    stacked = jnp.stack([member.astype(jnp.float32) for member in basis])
    local_c = jnp.sum(stacked * work[None], axis=1)
    coefs = reduce_small(local_c) / panels
    work = work - jnp.sum(coefs[:, None, :] * stacked, axis=0)
    square = reduce_small(jnp.sum(work * work, axis=0)) / panels
    beta = jnp.sqrt(square + 1e-06)
    fresh = (work / beta[None, :]).astype(jnp.bfloat16)
    return (fresh, [coefs[i] for i in range(len(basis))] + [beta])


def on_device(
    vector,
    self_term,
    near_blocks,
    near_rows,
    near_source,
    send_index,
    source_basis,
    target_basis,
    couplings,
    far_rows,
    far_cols,
):
    owned = source_basis.shape[0]
    cls = source_basis.shape[2]
    width = vector.shape[1]
    owners = lax.axis_size("blk")
    columns = lax.axis_size("col")
    rows_own = owned * cls
    panels = owners * rows_own
    share = rows_own // columns
    col_index = lax.axis_index("col")
    near_onehot = (near_rows[None, :] == jnp.arange(owned, dtype=jnp.int32)[:, None]).astype(
        jnp.float32
    )
    far_onehot = (far_rows[None, :] == jnp.arange(owned, dtype=jnp.int32)[:, None]).astype(
        jnp.float32
    )
    target_wide = target_basis.astype(jnp.float32)
    entries = []

    def reduce_owner(values):
        return lax.psum(values, "blk")

    basis = [vector]
    for step in range(ITERS):
        current = basis[-1]
        segs = current.reshape(owned, cls, width)
        padded = jnp.concatenate([segs, jnp.zeros((1, cls, width), jnp.bfloat16)], axis=0)
        outgoing = padded[send_index[0]]
        received = lax.all_to_all(outgoing, "blk", split_axis=0, concat_axis=0, tiled=True)
        sources = jnp.concatenate([segs, received], axis=0)
        picked = sources[near_source]
        products = jnp.einsum(
            "bij,bjw->biw", near_blocks, picked, preferred_element_type=jnp.float32
        )
        near_part = jnp.einsum(
            "rb,biw->riw", near_onehot, products, precision=lax.Precision.HIGHEST
        )
        coef = jnp.einsum(
            "krc,kcw->krw", source_basis, segs, preferred_element_type=jnp.float32
        ).astype(jnp.bfloat16)
        every = lax.all_gather(coef, "blk", axis=0, tiled=True)
        chosen = every[far_cols]
        mixed = jnp.einsum("fab,fbw->faw", couplings, chosen, preferred_element_type=jnp.float32)
        gathered_rows = jnp.einsum(
            "rf,faw->raw", far_onehot, mixed, precision=lax.Precision.HIGHEST
        )
        far_part = jnp.einsum(
            "kac,kaw->kcw", target_wide, gathered_rows, precision=lax.Precision.HIGHEST
        )
        work = lax.psum((near_part + far_part).reshape(rows_own, width), "col") + self_term[
            :, None
        ] * current.astype(jnp.float32)
        fresh, values = orthogonalize(work, basis, panels, reduce_owner)
        entries = entries + values
        basis.append(fresh)
    last_vector = lax.dynamic_slice_in_dim(basis[-1], col_index * share, share, 0)
    return (last_vector, jnp.stack(entries))


def solution(mesh):
    placed = (
        P(("grp", "blk"), "rhs"),
        P(("grp", "blk")),
        P(("grp", "blk", "col"), None, None),
        P(("grp", "blk", "col")),
        P(("grp", "blk", "col")),
        P(("grp", "blk"), None),
        P(("grp", "blk"), None, None),
        P(("grp", "blk"), None, None),
        P(("grp", "blk", "col"), None, None),
        P(("grp", "blk", "col")),
        P(("grp", "blk", "col")),
    )
    return jax.shard_map(
        on_device,
        mesh=mesh,
        in_specs=placed,
        out_specs=(P(("grp", "blk", "col"), "rhs"), P("grp", "rhs")),
        check_vma=False,
    )
```

profile of v0, /device:TPU:0, one launch (start us, length us, event | category | flops | bytes accessed | tf_op | source)
XLA Modules:
  0.0 296.3 jit_solution(5672359109752576407)
XLA Ops:
  7.2 0.7 fusion.22
  7.9 1.0 concatenate.18
  8.9 1.3 gather_fusion
  10.2 6.3 %all-to-all-start = ((bf16[4,256,128]{2,1,0:T(8,128)(2,1)}), bf16[4,256,128]{2,1,0:T(8,128)(2,1)S(1)}, u32[]{:S(2)}, u32[]{:S(2)}) async-start(bf16[4,256,128]{2,1,0:T(8,128)(2,1)} %gather_fusion), calls=%async_computation | async-start | bytes 524288 | tf_op jit(solution)/shard_map/all_to_all | solution.py:60
  16.5 1.2 convolution_convert_fusion.2
  17.6 15.0 %all_gather.9 = bf16[16,32,128]{2,1,0:T(8,128)(2,1)S(1)} all-gather(bf16[4,32,128]{2,1,0:T(8,128)(2,1)S(1)} %convolution_convert_fusion.2), channel_id=1, replica_groups=mesh['grp'=2,'blk'=4,'col'=2,'rhs'=2] {'blk'}, dimensions={0}, use_global_device_ids=true | all-gather | bytes 163840 | tf_op jit(solution)/shard_map/all_gather | solution.py:72
  32.7 0.8 copy.24
  33.5 0.7 gather_fusion.2
  34.5 1.0 fusion.6
  36.3 2.1 gather_fusion.1
  38.4 6.0 %convolution_bitcast_fusion.2 = f32[30,256,128]{1,2,0:T(8,128)} fusion(bf16[30,256,128]{2,1,0:T(8,128)(2,1)} %gather_fusion.1, bf16[30,256,256]{2,1,0:T(8,128)(2,1)} %param.13), kind=kOutput, calls=%fused_computation.11 | convolution fusion | flops 503316480 | bytes 9830400 | tf_op jit(solution)/shard_map/bij,bjw->biw/dot_general | solution.py:63
  44.4 5.5 %copy.23 = f32[30,256,128]{2,0,1:T(8,128)} copy(f32[30,256,128]{1,2,0:T(8,128)} %convolution_bitcast_fusion.2) | data formatting | bytes 7864320 | tf_op jit(solution)/shard_map/bij,bjw->biw/dot_general | solution.py:63
  49.9 3.6 %convolution_add_fusion.2 = f32[4,256,128]{2,0,1:T(4,128)S(1)} fusion(f32[30,256,128]{2,0,1:T(8,128)} %copy.23, f32[4,128,256]{1,0,2:T(4,128)S(1)} %copy.27, s32[30]{0:T(128)S(1)} %copy-done.6), kind=kOutput, calls=%fused_computation.20 | convolution fusion | flops 47317112 | bytes 4980856 | tf_op jit(solution)/shard_map/rb,biw->riw/dot_general | solution.py:66
  53.6 0.8 copy.28
  54.4 28.9 %all-reduce.7.cloned.1.call-done = f32[1024,128]{1,0:T(8,128)} async-done(((f32[1024,128]{1,0:T(8,128)}), f32[1024,128]{1,0:T(8,128)}) %all-reduce.7.cloned.1.call-update) | async-done | bytes 524304 | tf_op jit(solution)/shard_map/psum | solution.py:81
  83.3 1.3 fusion.11
  84.6 11.7 %psum.64 = f32[1,128]{1,0:T(1,128)S(1)} all-reduce(f32[1,128]{1,0:T(1,128)S(1)} %bitcast.93), channel_id=1, replica_groups=mesh['grp'=2,'blk'=4,'col'=2,'rhs'=2] {'blk'}, use_global_device_ids=true, to_apply=%region_2.0 | all-reduce | flops 128 | bytes 1024 | tf_op jit(solution)/shard_map/psum | solution.py:52
  96.3 1.3 multiply_reduce_fusion.6
  97.5 8.4 %psum.65 = f32[128]{0:T(128)S(1)} all-reduce(f32[128]{0:T(128)S(1)} %multiply_reduce_fusion.6), channel_id=1, replica_groups=mesh['grp'=2,'blk'=4,'col'=2,'rhs'=2] {'blk'}, use_global_device_ids=true, to_apply=%region_4.0 | all-reduce | flops 128 | bytes 1024 | tf_op jit(solution)/shard_map/psum | solution.py:52
  105.9 1.2 convert_bitcast_fusion.2
  107.4 1.3 gather_fusion.3
  108.7 3.4 %all-to-all-start.1 = ((bf16[4,256,128]{2,1,0:T(8,128)(2,1)}), bf16[4,256,128]{2,1,0:T(8,128)(2,1)S(1)}, u32[]{:S(2)}, u32[]{:S(2)}) async-start(bf16[4,256,128]{2,1,0:T(8,128)(2,1)} %gather_fusion.3), calls=%async_computation.1 | async-start | bytes 524288 | tf_op jit(solution)/shard_map/all_to_all | solution.py:60
  112.1 15.3 %all_gather.10 = bf16[16,32,128]{2,1,0:T(8,128)(2,1)S(1)} all-gather(bf16[4,32,128]{2,1,0:T(8,128)(2,1)S(1)} %fusion), channel_id=1, replica_groups=mesh['grp'=2,'blk'=4,'col'=2,'rhs'=2] {'blk'}, dimensions={0}, use_global_device_ids=true | all-gather | bytes 163840 | tf_op jit(solution)/shard_map/all_gather | solution.py:72
  128.4 1.0 fusion.4
  130.2 2.1 gather_fusion.4
  132.3 6.0 %convolution_bitcast_fusion.1 = f32[30,256,128]{1,2,0:T(8,128)} fusion(bf16[30,256,128]{2,1,0:T(8,128)(2,1)} %gather_fusion.4, bf16[30,256,256]{2,1,0:T(8,128)(2,1)} %param.13), kind=kOutput, calls=%fused_computation.10 | convolution fusion | flops 503316480 | bytes 9830400 | tf_op jit(solution)/shard_map/bij,bjw->biw/dot_general | solution.py:63
  138.3 5.5 %copy.30 = f32[30,256,128]{2,0,1:T(8,128)} copy(f32[30,256,128]{1,2,0:T(8,128)} %convolution_bitcast_fusion.1) | data formatting | bytes 7864320 | tf_op jit(solution)/shard_map/bij,bjw->biw/dot_general | solution.py:63
  143.8 3.6 %convolution_add_fusion.1 = f32[4,256,128]{2,0,1:T(4,128)S(1)} fusion(f32[30,256,128]{2,0,1:T(8,128)} %copy.30, f32[4,128,256]{1,0,2:T(4,128)S(1)} %copy.34, s32[30]{0:T(128)S(1)} %copy-done.6), kind=kOutput, calls=%fused_computation.19 | convolution fusion | flops 47317112 | bytes 4980856 | tf_op jit(solution)/shard_map/rb,biw->riw/dot_general | solution.py:66
  147.4 0.8 copy.35
  148.3 27.3 %all-reduce.9.cloned.1.call-done = f32[1024,128]{1,0:T(8,128)} async-done(((f32[1024,128]{1,0:T(8,128)}), f32[1024,128]{1,0:T(8,128)}) %all-reduce.9.cloned.1.call-update) | async-done | bytes 524304 | tf_op jit(solution)/shard_map/psum | solution.py:81
  175.6 1.2 fusion.8
  177.1 11.7 %psum.67 = f32[2,128]{1,0:T(2,128)S(1)} all-reduce(f32[2,128]{1,0:T(2,128)S(1)} %multiply_reduce_fusion.3), channel_id=1, replica_groups=mesh['grp'=2,'blk'=4,'col'=2,'rhs'=2] {'blk'}, use_global_device_ids=true, to_apply=%region_7.0 | all-reduce | flops 256 | bytes 2048 | tf_op jit(solution)/shard_map/psum | solution.py:52
  189.1 8.4 %psum.68 = f32[128]{0:T(128)S(1)} all-reduce(f32[128]{0:T(128)S(1)} %get-tuple-element.6), channel_id=1, replica_groups=mesh['grp'=2,'blk'=4,'col'=2,'rhs'=2] {'blk'}, use_global_device_ids=true, to_apply=%region_10.0 | all-reduce | flops 128 | bytes 1024 | tf_op jit(solution)/shard_map/psum | solution.py:52
  197.7 1.3 gather_fusion.6
  199.0 3.4 %all-to-all-start.2 = ((bf16[4,256,128]{2,1,0:T(8,128)(2,1)}), bf16[4,256,128]{2,1,0:T(8,128)(2,1)S(1)}, u32[]{:S(2)}, u32[]{:S(2)}) async-start(bf16[4,256,128]{2,1,0:T(8,128)(2,1)} %gather_fusion.6), calls=%async_computation.2 | async-start | bytes 524288 | tf_op jit(solution)/shard_map/all_to_all | solution.py:60
  202.5 15.4 %all_gather.11 = bf16[16,32,128]{2,1,0:T(8,128)(2,1)S(1)} all-gather(bf16[4,32,128]{2,1,0:T(8,128)(2,1)S(1)} %fusion.1), channel_id=1, replica_groups=mesh['grp'=2,'blk'=4,'col'=2,'rhs'=2] {'blk'}, dimensions={0}, use_global_device_ids=true | all-gather | bytes 163840 | tf_op jit(solution)/shard_map/all_gather | solution.py:72
  218.8 1.0 fusion.2
  220.6 2.1 gather_fusion.7
  222.7 6.0 %convolution_bitcast_fusion = f32[30,256,128]{1,2,0:T(8,128)} fusion(bf16[30,256,128]{2,1,0:T(8,128)(2,1)} %gather_fusion.7, bf16[30,256,256]{2,1,0:T(8,128)(2,1)} %param.13), kind=kOutput, calls=%fused_computation.9 | convolution fusion | flops 503316480 | bytes 9830400 | tf_op jit(solution)/shard_map/bij,bjw->biw/dot_general | solution.py:63
  228.7 5.5 %copy.37 = f32[30,256,128]{2,0,1:T(8,128)} copy(f32[30,256,128]{1,2,0:T(8,128)} %convolution_bitcast_fusion) | data formatting | bytes 7864320 | tf_op jit(solution)/shard_map/bij,bjw->biw/dot_general | solution.py:63
  234.2 3.6 %convolution_add_fusion = f32[4,256,128]{2,0,1:T(4,128)S(1)} fusion(f32[30,256,128]{2,0,1:T(8,128)} %copy.37, f32[4,128,256]{1,0,2:T(4,128)S(1)} %copy.41, s32[30]{0:T(128)S(1)} %copy-done.6), kind=kOutput, calls=%fused_computation.18 | convolution fusion | flops 47317112 | bytes 4980856 | tf_op jit(solution)/shard_map/rb,biw->riw/dot_general | solution.py:66
  237.8 0.8 copy.42
  238.7 27.4 %all-reduce.11.cloned.1.call-done = f32[1024,128]{1,0:T(8,128)} async-done(((f32[1024,128]{1,0:T(8,128)}), f32[1024,128]{1,0:T(8,128)}) %all-reduce.11.cloned.1.call-update) | async-done | bytes 524304 | tf_op jit(solution)/shard_map/psum | solution.py:81
  266.0 1.2 fusion.9
  267.5 11.7 %psum.70 = f32[3,128]{1,0:T(4,128)S(1)} all-reduce(f32[3,128]{1,0:T(4,128)S(1)} %multiply_reduce_fusion.1), channel_id=1, replica_groups=mesh['grp'=2,'blk'=4,'col'=2,'rhs'=2] {'blk'}, use_global_device_ids=true, to_apply=%region_13.0 | all-reduce | flops 384 | bytes 3072 | tf_op jit(solution)/shard_map/psum | solution.py:52
  279.5 8.4 %psum.71 = f32[128]{0:T(128)S(1)} all-reduce(f32[128]{0:T(128)S(1)} %get-tuple-element.2), channel_id=1, replica_groups=mesh['grp'=2,'blk'=4,'col'=2,'rhs'=2] {'blk'}, use_global_device_ids=true, to_apply=%region_16.0 | all-reduce | flops 128 | bytes 1024 | tf_op jit(solution)/shard_map/psum | solution.py:52
  287.8 0.7 fusion.13
  288.5 1.2 stack.30
  (64 shorter events, 6.0 us)
Async XLA Ops:
  7.2 28.4 %copy-start = (bf16[4,32,256]{2,1,0:T(8,128)(2,1)S(1)}, bf16[4,32,256]{2,1,0:T(8,128)(2,1)}, u32[]{:S(2)}) copy-start(bf16[4,32,256]{2,1,0:T(8,128)(2,1)} %param.18) | copy-start | bytes 196612
  7.2 25.5 %copy-start.7 = (s32[64]{0:T(128)S(1)}, s32[64]{0:T(128)}, u32[]{:S(2)}) copy-start(s32[64]{0:T(128)} %param.21) | copy-start | bytes 772
  7.2 25.5 %copy-start.3 = (bf16[64,32,32]{0,2,1:T(8,128)(2,1)S(1)}, bf16[64,32,32]{0,2,1:T(8,128)(2,1)}, u32[]{:S(2)}) copy-start(bf16[64,32,32]{0,2,1:T(8,128)(2,1)} %param.19) | copy-start | bytes 393220
  10.2 26.1 %all-to-all-start = ((bf16[4,256,128]{2,1,0:T(8,128)(2,1)}), bf16[4,256,128]{2,1,0:T(8,128)(2,1)S(1)}, u32[]{:S(2)}, u32[]{:S(2)}) async-start(bf16[4,256,128]{2,1,0:T(8,128)(2,1)} %gather_fusion), calls=%async_computation | async-start | bytes 524288 | tf_op jit(solution)/shard_map/all_to_all | solution.py:60
  16.5 66.8 %all-reduce.7.cloned.1.call-start = ((), (), s32[]{:S(2)}) async-start(), calls=%async_computation.3 | async-start | bytes 1048576 | tf_op jit(solution)/shard_map/psum | solution.py:81
  32.7 1.8 copy-start.5
  34.2 2.0 copy-start.8
  34.2 2.1 copy-start.1
  44.4 5.5 %copy-start.6 = (s32[30]{0:T(128)S(1)}, s32[30]{0:T(128)}, u32[]{:S(2)}) copy-start(s32[30]{0:T(128)} %param.14) | copy-start | bytes 364
  49.9 33.4 %copy-start.4 = (f32[1024]{0:T(1024)S(1)}, f32[1024]{0:T(1024)}, u32[]{:S(2)}) copy-start(f32[1024]{0:T(1024)} %param.12) | copy-start | bytes 12292
  54.4 52.8 %copy-start.2 = (bf16[4,32,256]{2,1,0:T(8,128)(2,1)S(1)}, bf16[4,32,256]{2,1,0:T(8,128)(2,1)}, u32[]{:S(2)}) copy-start(bf16[4,32,256]{2,1,0:T(8,128)(2,1)} %param.17) | copy-start | bytes 196612
  108.7 21.5 %all-to-all-start.1 = ((bf16[4,256,128]{2,1,0:T(8,128)(2,1)}), bf16[4,256,128]{2,1,0:T(8,128)(2,1)S(1)}, u32[]{:S(2)}, u32[]{:S(2)}) async-start(bf16[4,256,128]{2,1,0:T(8,128)(2,1)} %gather_fusion.3), calls=%async_computation.1 | async-start | bytes 524288 | tf_op jit(solution)/shard_map/all_to_all | solution.py:60
  112.1 63.6 %all-reduce.9.cloned.1.call-start = ((), (), s32[]{:S(2)}) async-start(), calls=%async_computation.4 | async-start | bytes 1048576 | tf_op jit(solution)/shard_map/psum | solution.py:81
  199.0 21.5 %all-to-all-start.2 = ((bf16[4,256,128]{2,1,0:T(8,128)(2,1)}), bf16[4,256,128]{2,1,0:T(8,128)(2,1)S(1)}, u32[]{:S(2)}, u32[]{:S(2)}) async-start(bf16[4,256,128]{2,1,0:T(8,128)(2,1)} %gather_fusion.6), calls=%async_computation.2 | async-start | bytes 524288 | tf_op jit(solution)/shard_map/all_to_all | solution.py:60
  202.4 63.6 %all-reduce.11.cloned.1.call-start = ((), (), s32[]{:S(2)}) async-start(), calls=%async_computation.5 | async-start | bytes 1048576 | tf_op jit(solution)/shard_map/psum | solution.py:81
Sparse Core Ops, SparseCore 0:
  54.5 28.7 all-reduce.6
  148.4 27.1 all-reduce.8
  238.8 27.2 all-reduce.10
where the time goes:
time: 297 us; the launch traced here: 296 us
  blocking collectives  106 us (36%)
  waiting for transfers between devices  83.6 us (28%)
  matrix products  35.6 us (12%)
  local copies, waits for them, and re-layouts  34.9 us (12%)
  between operations  14.1 us (5%)
  starting transfers between devices  13.2 us (4%)
  other arithmetic  8.94 us (3%)
    psum x3, waiting for transfers between devices, on_device(): lax.psum((near_part + far_part).reshape(rows_own, width), 'col')  83.6 us
    psum x6, blocking collectives, reduce_owner(): return lax.psum(values, 'blk')  60.2 us
    all_gather x3, blocking collectives, on_device(): every = lax.all_gather(coef, 'blk', axis=0, tiled=True)  45.8 us
    dot_general x3, matrix products, on_device(): jnp.einsum('bij,bjw->biw', near_blocks, picked, preferred_element_type=jn...  18 us
    dot_general x3, local copies, waits for them, and re-layouts, on_device(): jnp.einsum('bij,bjw->biw', near_blocks, picked, preferred_element_type=jn...  16.5 us
    all_to_all x3, starting transfers between devices, on_device(): lax.all_to_all(outgoing, 'blk', split_axis=0, concat_axis=0, tiled=True)  13.1 us
    dot_general x3, matrix products, on_device(): jnp.einsum('rb,biw->riw', near_onehot, products, precision=lax.Precision....  10.9 us
    gather x3, local copies, waits for them, and re-layouts, on_device(): picked = sources[near_source]  6.28 us
  transfers between devices with their start and end apart: 6, of which 3 were waited for; matrix products, arithmetic and copies ran while one was open for 3% of the time, Pallas kernels for 0%

commit v1 on v0

v1 whole, which is shorter than its diff:
```python
import functools

import jax
import jax.numpy as jnp
from jax import lax
from jax.experimental import pallas as pl
from jax.experimental.pallas import tpu as pltpu
from jax.sharding import PartitionSpec as P

ITERS = 3
MESH = pl.DeviceIdType.MESH


def dot(a, b):
    return jnp.dot(a, b, preferred_element_type=jnp.float32)


def pack_kernel(rows_ref, cols_ref, frows_ref, fcols_ref, near_ref, coup_ref, target_ref,
                dense_ref, far_ref, lift_ref, cells):
    cls = near_ref.shape[1]
    rank = coup_ref.shape[1]
    dense_ref[...] = jnp.zeros_like(dense_ref)
    cells[...] = jnp.zeros_like(cells)

    @pl.loop(0, near_ref.shape[0])
    def _(b):
        where = (rows_ref[b], slice(None), pl.ds(pl.multiple_of(cols_ref[b] * cls, cls), cls))
        dense_ref[where] += near_ref[b]

    @pl.loop(0, coup_ref.shape[0])
    def _(f):
        at = pl.ds(pl.multiple_of(frows_ref[f] * rank, rank), rank)
        cells[fcols_ref[f], at, :] += coup_ref[f].astype(jnp.float32)

    for c in range(cells.shape[0]):
        far_ref[:, c * rank:(c + 1) * rank] = cells[c].astype(jnp.bfloat16)
    for r in range(target_ref.shape[0]):
        lift_ref[r] = target_ref[r].astype(jnp.float32).T.astype(jnp.bfloat16)


def solve_kernel(n, ncol, send_ref, vector_ref, self_ref, dense_ref, far_ref, source_ref, lift_ref,
                 last_ref, hess_ref,
                 basis, work, seg_out, seg_in, coef, parts, dots,
                 seg_s, seg_r, coef_s, coef_r, part_s, part_r, dot_s, dot_r):
    me = lax.axis_index("blk")
    mycol = lax.axis_index("col")
    owned, cls, width = vector_ref.shape
    rank = source_ref.shape[1]
    panels = n * owned * cls
    barrier = pltpu.get_barrier_semaphore()
    for j in range(1, n):
        pl.semaphore_signal(barrier, inc=1, device_id={"blk": lax.rem(me + j, n)}, device_id_type=MESH)
    for j in range(1, ncol):
        pl.semaphore_signal(barrier, inc=1, device_id={"col": lax.rem(mycol + j, ncol)}, device_id_type=MESH)
    pl.semaphore_wait(barrier, n - 1 + ncol - 1)

    pending = []
    gram = {}
    line = 0

    def member(i):
        return vector_ref if i == 0 else basis.at[i - 1]

    def send(src, dst, ssem, rsem, axis, peer):
        copy = pltpu.make_async_remote_copy(src_ref=src, dst_ref=dst, send_sem=ssem, recv_sem=rsem,
                                            device_id={axis: peer}, device_id_type=MESH)
        copy.start()
        pending.append(copy)

    def arrived(dst, rsem):
        pltpu.make_async_copy(dst, dst, rsem).wait()

    for step in range(ITERS):
        current = member(step)
        for j in range(1, n):
            peer = lax.rem(me + j, n)
            pick = jnp.minimum(send_ref[0, peer], owned - 1)
            seg_out[step, j - 1] = current[pick]
            send(seg_out.at[step, j - 1], seg_in.at[step, n - j - 1],
                 seg_s.at[step, j - 1], seg_r.at[step, n - j - 1], "blk", peer)
        for c in range(owned):
            coef[step, me, c * rank:(c + 1) * rank, :] = dot(source_ref[c], current[c]).astype(jnp.bfloat16)
        for j in range(1, n):
            send(coef.at[step, me], coef.at[step, me], coef_s.at[step, j - 1], coef_r.at[step, n - j - 1],
                 "blk", lax.rem(me + j, n))
        mine = current[...].reshape(owned * cls, width)
        for r in range(owned):
            work[r] = dot(dense_ref[r, :, :owned * cls], mine)
        for j in range(1, n):
            arrived(coef.at[step, lax.rem(me + j, n)], coef_r.at[step, j - 1])
        zeta = dot(far_ref[...], coef[step].reshape(n * owned * rank, width)).astype(jnp.bfloat16)
        for j in range(1, n):
            arrived(seg_in.at[step, j - 1], seg_r.at[step, j - 1])
        theirs = seg_in[step].reshape((n - 1) * cls, width)
        for r in range(owned):
            total = work[r] + dot(dense_ref[r, :, owned * cls:], theirs)
            total = total + dot(lift_ref[r], zeta[r * rank:(r + 1) * rank])
            parts[step, r, mycol] = total.astype(jnp.bfloat16)
            for j in range(1, ncol):
                send(parts.at[step, r, mycol], parts.at[step, r, mycol],
                     part_s.at[step, r, j - 1], part_r.at[step, r, ncol - j - 1],
                     "col", lax.rem(mycol + j, ncol))
        count = step + 1
        sums = [0.0] * (2 * count + 1)
        for r in range(owned):
            newest = current[r].astype(jnp.float32)
            for i in range(count):
                other = newest if i == step else member(i)[r].astype(jnp.float32)
                sums[count + 1 + i] += jnp.sum(newest * other, axis=0, keepdims=True)
        for r in range(owned):
            for j in range(1, ncol):
                arrived(parts.at[step, r, lax.rem(mycol + j, ncol)], part_r.at[step, r, j - 1])
            total = self_ref[r] * current[r].astype(jnp.float32)
            for k in range(ncol):
                total = total + parts[step, r, k].astype(jnp.float32)
            work[r] = total
            for i in range(count):
                sums[i] += jnp.sum(total * member(i)[r].astype(jnp.float32), axis=0, keepdims=True)
            sums[count] += jnp.sum(total * total, axis=0, keepdims=True)
        pad = [jnp.zeros((1, width), jnp.float32)] * (8 - len(sums))
        dots[step, me] = jnp.concatenate(sums + pad, axis=0)
        for j in range(1, n):
            send(dots.at[step, me], dots.at[step, me], dot_s.at[step, j - 1], dot_r.at[step, n - j - 1],
                 "blk", lax.rem(me + j, n))
        for j in range(1, n):
            arrived(dots.at[step, lax.rem(me + j, n)], dot_r.at[step, j - 1])
        total = dots[step, 0]
        for k in range(1, n):
            total = total + dots[step, k]
        total = total / panels
        coefs = [total[i:i + 1] for i in range(count)]
        for i in range(count):
            gram[i, step] = gram[step, i] = total[count + 1 + i:count + 2 + i]
        square = total[count:count + 1]
        for i in range(count):
            inner = -2.0 * coefs[i]
            for k in range(count):
                inner = inner + coefs[k] * gram[i, k]
            square = square + coefs[i] * inner
        beta = jnp.sqrt(jnp.maximum(square, 0.0) + 1e-06)
        scale = 1.0 / beta
        for value in coefs + [beta]:
            hess_ref[line:line + 1, :] = value
            line += 1
        if step < ITERS - 1:
            for r in range(owned):
                fresh = work[r]
                for i in range(count):
                    fresh = fresh - coefs[i] * member(i)[r].astype(jnp.float32)
                basis[step, r] = (fresh * scale).astype(jnp.bfloat16)
        else:
            share = owned * cls // ncol
            at = pl.multiple_of(mycol * share, share)
            fresh = work.reshape(owned * cls, width)[pl.ds(at, share)]
            for i in range(count):
                fresh = fresh - coefs[i] * member(i).reshape(owned * cls, width)[pl.ds(at, share)].astype(jnp.float32)
            last_ref[...] = (fresh * scale).astype(jnp.bfloat16)
    for copy in pending:
        copy.wait_send()


def on_device(vector, self_term, near_blocks, near_rows, near_source, send_index, source_basis,
              target_basis, couplings, far_rows, far_cols):
    owned, rank, cls = source_basis.shape
    width = vector.shape[1]
    n = lax.axis_size("blk")
    ncol = lax.axis_size("col")
    me = lax.axis_index("blk")
    clusters = n * owned
    sources = owned + n - 1
    bf16, f32 = jnp.bfloat16, jnp.float32
    place = jnp.where(near_source < owned, near_source,
                      owned - 1 + lax.rem(near_source - owned - me + n, n))
    vmem, smem = pl.BlockSpec(memory_space=pltpu.VMEM), pl.BlockSpec(memory_space=pltpu.SMEM)
    dense, far, lift = pl.pallas_call(
        pack_kernel,
        out_shape=(
            jax.ShapeDtypeStruct((owned, cls, sources * cls), bf16),
            jax.ShapeDtypeStruct((owned * rank, clusters * rank), bf16),
            jax.ShapeDtypeStruct((owned, cls, rank), bf16),
        ),
        in_specs=[smem] * 4 + [vmem] * 3,
        out_specs=(vmem,) * 3,
        scratch_shapes=[pltpu.VMEM((clusters, owned * rank, rank), f32)],
        compiler_params=pltpu.CompilerParams(vmem_limit_bytes=50 << 20),
        name="pack",
    )(near_rows, place, far_rows, far_cols, near_blocks, couplings, target_basis)
    dma = pltpu.SemaphoreType.DMA
    wide_self = jnp.broadcast_to(self_term.reshape(owned, cls, 1), (owned, cls, width))
    return pl.pallas_call(
        functools.partial(solve_kernel, n, ncol),
        out_shape=(
            jax.ShapeDtypeStruct((owned * cls // ncol, width), bf16),
            jax.ShapeDtypeStruct((ITERS * (ITERS + 3) // 2, width), f32),
        ),
        in_specs=[smem] + [vmem] * 6,
        out_specs=(vmem, vmem),
        scratch_shapes=[
            pltpu.VMEM((ITERS - 1, owned, cls, width), bf16),
            pltpu.VMEM((owned, cls, width), f32),
            pltpu.VMEM((ITERS, n - 1, cls, width), bf16),
            pltpu.VMEM((ITERS, n - 1, cls, width), bf16),
            pltpu.VMEM((ITERS, n, owned * rank, width), bf16),
            pltpu.VMEM((ITERS, owned, ncol, cls, width), bf16),
            pltpu.VMEM((ITERS, n, 8, width), f32),
            dma((ITERS, n - 1)), dma((ITERS, n - 1)),
            dma((ITERS, n - 1)), dma((ITERS, n - 1)),
            dma((ITERS, owned, ncol - 1)), dma((ITERS, owned, ncol - 1)),
            dma((ITERS, n - 1)), dma((ITERS, n - 1)),
        ],
        compiler_params=pltpu.CompilerParams(collective_id=0, has_side_effects=True, vmem_limit_bytes=50 << 20),
        name="solve",
    )(send_index, vector.reshape(owned, cls, width), wide_self, dense, far, source_basis, lift)


def solution(mesh):
    placed = (
        P(("grp", "blk"), "rhs"),
        P(("grp", "blk")),
        P(("grp", "blk", "col"), None, None),
        P(("grp", "blk", "col")),
        P(("grp", "blk", "col")),
        P(("grp", "blk"), None),
        P(("grp", "blk"), None, None),
        P(("grp", "blk"), None, None),
        P(("grp", "blk", "col"), None, None),
        P(("grp", "blk", "col")),
        P(("grp", "blk", "col")),
    )
    return jax.shard_map(
        on_device,
        mesh=mesh,
        in_specs=placed,
        out_specs=(P(("grp", "blk", "col"), "rhs"), P("grp", "rhs")),
        check_vma=False,
    )
```

time: 297 us -> 76.9 us (0.26)
  blocking collectives: 106 us -> 0 us
  waiting for transfers between devices: 83.6 us -> 0 us
  Pallas kernels: 0 us -> 69.2 us
  matrix products: 35.6 us -> 0 us
  local copies, waits for them, and re-layouts: 34.9 us -> 6.04 us
  between operations: 14.1 us -> 0.72 us
  starting transfers between devices: 13.2 us -> 0 us
  other arithmetic: 8.94 us -> 0.67 us
    psum x3 -> x0, waiting for transfers between devices: 83.6 us -> none  [on_device(): lax.psum((near_part + far_part).reshape(rows_own, width), 'col')]
    pallas_call x0 -> x2, Pallas kernels: none -> 69.2 us  [the longest x1 63.7 us: on_device(): pl.pallas_call(functools.partial(solve_kernel, n, ncol), out_shape=(jax.S...]
    psum x6 -> x0, blocking collectives: 60.2 us -> none  [reduce_owner(): return lax.psum(values, 'blk')]
    all_gather x3 -> x0, blocking collectives: 45.8 us -> none  [on_device(): every = lax.all_gather(coef, 'blk', axis=0, tiled=True)]
    dot_general x18 -> x0, matrix products: 35.6 us -> none  [the longest x3 18 us: on_device(): jnp.einsum('bij,bjw->biw', near_blocks, picked, preferred_element_type=jn...]
    dot_general x6 -> x0, local copies, waits for them, and re-layouts: 17.2 us -> none  [the longest x3 16.5 us: on_device(): jnp.einsum('bij,bjw->biw', near_blocks, picked, preferred_element_type=jn...]
    all_to_all x3 -> x0, starting transfers between devices: 13.1 us -> none  [on_device(): lax.all_to_all(outgoing, 'blk', split_axis=0, concat_axis=0, tiled=True)]
    gather x9 -> x0, local copies, waits for them, and re-layouts: 12.1 us -> none  [the longest x3 6.28 us: on_device(): picked = sources[near_source]]
  transfers between devices with their start and end apart: 6 -> 0, of which waited for: 3 -> 0; matrix products, arithmetic and copies ran while one was open for 3% -> 0% of each run, Pallas kernels for 0% -> 0%
where the time goes in v1:
time: 76.9 us; the launch traced here: 76.6 us
  Pallas kernels  69.2 us (90%)
  local copies, waits for them, and re-layouts  6.04 us (8%)
    pallas_call x1, Pallas kernels, on_device(): pl.pallas_call(functools.partial(solve_kernel, n, ncol), out_shape=(jax.S...  63.7 us
    unnamed x19, local copies, waits for them, and re-layouts  5.84 us
    pallas_call x1, Pallas kernels, on_device(): pl.pallas_call(pack_kernel, out_shape=(jax.ShapeDtypeStruct((owned, cls,...  5.5 us

profile of v1, /device:TPU:0, one launch (start us, length us, event | category | flops | bytes accessed | tf_op | source)
XLA Modules:
  0.0 76.6 jit_solution(72422246951198201)
XLA Ops:
  0.6 0.0 copy-start.7
  0.6 0.0 copy-start
  0.7 0.0 copy-start.6
  0.7 0.0 copy-start.2
  0.7 1.8 %copy.13.coup_ref = bf16[64,32,32]{2,1,0:T(8,128)(2,1)S(1)} copy(bf16[64,32,32]{0,2,1:T(8,128)(2,1)} %param.19) | data formatting | bytes 262144 | tf_op args[8]
  2.4 0.7 compare_select_fusion.cols_ref
  3.1 0.0 copy-start.1
  3.1 0.8 %copy-done.1 = bf16[4,32,256]{2,1,0:T(8,128)(2,1)S(1)} copy-done((bf16[4,32,256]{2,1,0:T(8,128)(2,1)S(1)}, bf16[4,32,256]{2,1,0:T(8,128)(2,1)}, u32[]{:S(2)}) %copy-start.1) | copy-done | bytes 65560
  4.0 0.0 copy-start.3
  4.0 0.7 copy-done.3
  4.6 0.0 copy-start.4
  4.6 0.7 copy-done.4
  5.3 0.0 copy-start.5
  5.3 0.7 copy-done.5
  5.9 5.5 %pack.1 = (bf16[4,256,1792]{2,1,0:T(8,128)(2,1)}, bf16[128,512]{1,0:T(8,128)(2,1)S(1)}, bf16[4,256,32]{2,1,0:T(8,128)(2,1)S(1)}) custom-call(s32[30]{0:T(128)S(1)} %copy-done.3, s32[30]{0:T(128)S(1)} %compare_select_fusion.cols_ref, s32[64]{0:T(128)S(1)} %copy-done.4, s32[64]{0:T(128)S(1)} %copy-done.5, bf16[30,256,256]{2,1,0:T(8,128)(2,1)} %near_ref.1, ...), custom_call_target="tpu_custom_call" | custom-call | tf_op jit(solution)/shard_map/pack/pallas_call | solution.py:175
  11.4 0.0 copy-done.7
  11.4 0.2 broadcast_in_dim.8.self_ref
  11.6 0.0 copy-done
  11.6 0.0 copy-done.6
  11.6 0.0 copy-done.2
  11.7 63.7 %solve.1 = (bf16[512,128]{1,0:T(8,128)(2,1)S(1)}, f32[9,128]{1,0:T(8,128)S(1)}) custom-call(s32[1,4]{1,0:T(1,128)S(1)} %copy-done.6, bf16[4,256,128]{2,1,0:T(8,128)(2,1)S(1)} %bitcast.1, f32[4,256,128]{2,1,0:T(8,128)S(1)} %broadcast_in_dim.8.self_ref, bf16[4,256,1792]{2,1,0:T(8,128)(2,1)} %get-tuple-element.5.dense_ref, ...), custom_call_target="tpu_custom_call" | custom-call | tf_op jit(solution)/shard_map/solve/pallas_call | solution.py:190
  75.4 0.7 copy.16
  76.0 0.6 copy.17
  (1 shorter events, 0.0 us)
Async XLA Ops:
  0.6 10.8 %copy-start.7 = (f32[1024]{0:T(1024)S(1)}, f32[1024]{0:T(1024)}, u32[]{:S(2)}) copy-start(f32[1024]{0:T(1024)} %param.12) | copy-start | bytes 12292
  0.6 11.0 %copy-start = (bf16[1024,128]{1,0:T(8,128)(2,1)S(1)}, bf16[1024,128]{1,0:T(8,128)(2,1)}, u32[]{:S(2)}) copy-start(bf16[1024,128]{1,0:T(8,128)(2,1)} %param.11) | copy-start | bytes 786436
  0.7 11.0 %copy-start.6 = (s32[1,4]{1,0:T(1,128)S(1)}, s32[1,4]{1,0:T(1,128)}, u32[]{:S(2)}) copy-start(s32[1,4]{1,0:T(1,128)} %send_ref.1) | copy-start | bytes 52
  0.7 11.0 %copy-start.2 = (bf16[4,32,256]{2,1,0:T(8,128)(2,1)S(1)}, bf16[4,32,256]{2,1,0:T(8,128)(2,1)}, u32[]{:S(2)}) copy-start(bf16[4,32,256]{2,1,0:T(8,128)(2,1)} %source_ref.1) | copy-start | bytes 196612
  3.1 0.8 %copy-start.1 = (bf16[4,32,256]{2,1,0:T(8,128)(2,1)S(1)}, bf16[4,32,256]{2,1,0:T(8,128)(2,1)}, u32[]{:S(2)}) copy-start(bf16[4,32,256]{2,1,0:T(8,128)(2,1)} %target_ref.1) | copy-start | bytes 196612
  4.0 0.7 copy-start.3
  4.6 0.7 copy-start.4
  5.3 0.7 copy-start.5

commit v2 on v1

v2 whole, which is shorter than its diff:
```python
import functools

import jax
import jax.numpy as jnp
from jax import lax
from jax.experimental import pallas as pl
from jax.experimental.pallas import tpu as pltpu
from jax.sharding import PartitionSpec as P

ITERS = 3
MESH = pl.DeviceIdType.MESH


def dot(a, b):
    return jnp.dot(a, b, preferred_element_type=jnp.float32)


def pack(n, rows, cols, near_in, coup_ref, frows_ref, target_ref, cells, keys, turned, dense, far, lift, near_sem):
    me = lax.axis_index("blk")
    count, cls, _ = near_in.shape
    owned = target_ref.shape[0]
    rank = turned.shape[0]
    sources = owned + n - 1
    fetch = pltpu.make_async_copy(near_in, cells.at[pl.ds(0, count)], near_sem)
    fetch.start()
    cells[count] = jnp.zeros((cls, cls), jnp.bfloat16)
    for b in range(count):
        source = cols[b]
        place = jnp.where(source < owned, source, owned - 1 + lax.rem(source - owned - me + n, n))
        keys[b] = rows[b] * sources + place

    for k in range(rank):
        turned[k] = coup_ref[k].astype(jnp.float32).T
    per = 128 // rank
    lane = lax.broadcasted_iota(jnp.int32, (rank, 128), 1)
    for g in range(frows_ref.shape[0] // per):
        wide = jnp.concatenate([turned[:, g * per + i, :] for i in range(per)], axis=1)
        row = jnp.full((rank, 128), frows_ref[g * per], jnp.int32)
        for i in range(1, per):
            row = jnp.where(lane >= i * rank, frows_ref[g * per + i], row)
        for r in range(owned):
            far[r * rank:(r + 1) * rank, g * 128:(g + 1) * 128] = jnp.where(row == r, wide, 0.0).astype(jnp.bfloat16)
    for r in range(owned):
        lift[r] = target_ref[r].astype(jnp.float32).T.astype(jnp.bfloat16)

    def latest(key, limit):
        found = jnp.int32(count)
        for b in range(count):
            hit = keys[b] == key
            if limit is not None:
                hit = jnp.logical_and(hit, b < limit)
            found = jnp.where(hit, b, found)
        return found

    fetch.wait()

    @pl.loop(0, count)
    def _(b):
        cells[b] = cells[b] + cells[latest(keys[b], b)]

    @pl.loop(0, owned)
    def _(r):
        for c in range(sources):
            dense[r, :, c * cls:(c + 1) * cls] = cells[latest(r * sources + c, None)]


def solve_kernel(n, ncol, rows, cols, send_ref, frows_ref, fcols_ref, near_in, vector_ref, self_ref,
                 source_ref, target_ref, coup_ref,
                 last_ref, hess_ref,
                 cells, keys, turned, dense, far, lift,
                 basis, work, outgoing, incoming, seg, raw, coef, chosen, parts, dots,
                 near_sem, out_s, in_r, fwd_s, fwd_r, part_s, part_r, dot_s, dot_r):
    me = lax.axis_index("blk")
    mycol = lax.axis_index("col")
    owned, cls, width = vector_ref.shape
    rank = source_ref.shape[1]
    panels = n * owned * cls
    block = owned * rank
    share, cshare = cls // ncol, block // ncol
    everyone = [(j, c) for j in range(n) for c in range(ncol) if j or c]
    barrier = pltpu.get_barrier_semaphore()

    def at(j, c):
        return {"blk": lax.rem(me + j, n), "col": lax.rem(mycol + c, ncol)}

    for j, c in everyone:
        pl.semaphore_signal(barrier, inc=1, device_id=at(j, c), device_id_type=MESH)
    pl.semaphore_wait(barrier, len(everyone))

    pending = []
    gram = {}
    line = 0

    def member(i):
        return vector_ref if i == 0 else basis.at[i - 1]

    def send(src, dst, ssem, rsem, j, c):
        copy = pltpu.make_async_remote_copy(src_ref=src, dst_ref=dst, send_sem=ssem, recv_sem=rsem,
                                            device_id=at(j, c), device_id_type=MESH)
        copy.start()
        pending.append(copy)

    def arrived(dst, rsem):
        pltpu.make_async_copy(dst, dst, rsem).wait()

    def owner_rows(j):
        return pl.multiple_of(lax.rem(me + j, n) * block, block)

    def share_out(step, field):
        for c in range(owned):
            raw[pl.ds(owner_rows(0) + c * rank, rank), :] = dot(
                source_ref[c], field[c].astype(jnp.bfloat16)).astype(jnp.bfloat16)
        mine = raw[pl.ds(pl.multiple_of(owner_rows(0) + mycol * cshare, cshare), cshare), :]
        for j in range(1, n):
            pick = jnp.minimum(send_ref[0, lax.rem(me + j, n)], owned - 1)
            outgoing[step, j - 1, :share] = field[pick, pl.ds(pl.multiple_of(mycol * share, share), share), :].astype(jnp.bfloat16)
            outgoing[step, j - 1, share:] = mine
            send(outgoing.at[step, j - 1], incoming.at[step, n - j - 1, mycol],
                 out_s.at[step, j - 1], in_r.at[step, n - j - 1], j, 0)

    def pass_on(step):
        for j in range(1, n):
            here = incoming.at[step, j - 1, mycol]
            arrived(here, in_r.at[step, j - 1])
            for c in range(1, ncol):
                send(here, here, fwd_s.at[step, j - 1, c - 1], fwd_r.at[step, j - 1, ncol - c - 1], 0, c)

    def collect(step):
        for j in range(1, n):
            for c in range(1, ncol):
                arrived(incoming.at[step, j - 1, lax.rem(mycol + c, ncol)], fwd_r.at[step, j - 1, c - 1])
            for k in range(ncol):
                seg[step, j - 1, k * share:(k + 1) * share] = incoming[step, j - 1, k, :share]
                raw[pl.ds(pl.multiple_of(owner_rows(j) + k * cshare, cshare), cshare), :] = incoming[step, j - 1, k, share:]

    share_out(0, vector_ref)
    pack(n, rows, cols, near_in, coup_ref, frows_ref, target_ref, cells, keys, turned, dense, far, lift, near_sem)
    coefs, scale = [], None
    for step in range(ITERS):
        current = member(step)
        final = step == ITERS - 1
        pass_on(step)
        mine = current[...].reshape(owned * cls, width)
        for r in range(owned):
            work[r] = dot(dense[r, :, :owned * cls], mine)
        collect(step)
        if step == 0:
            coef[0] = raw[...].reshape(n * owned, rank, width)
        else:
            fresh = raw[...].reshape(n * owned, rank, width).astype(jnp.float32)
            for i in range(step):
                fresh = fresh - coefs[i] * coef[i].astype(jnp.float32)
            coef[step] = (fresh * scale).astype(jnp.bfloat16)
            for j in range(n - 1):
                fresh = seg[step, j].astype(jnp.float32)
                for i in range(step):
                    fresh = fresh - coefs[i] * seg[i, j].astype(jnp.float32)
                seg[step, j] = (fresh * scale).astype(jnp.bfloat16)
        for f in range(fcols_ref.shape[0]):
            chosen[f * rank:(f + 1) * rank] = coef[step, fcols_ref[f]]
        zeta = dot(far[...], chosen[...]).astype(jnp.bfloat16)
        chosen[:block] = zeta
        theirs = seg[step].reshape((n - 1) * cls, width)

        def total_of(r):
            total = work[r] + dot(dense[r, :, owned * cls:], theirs)
            zeta_r = chosen[pl.ds(pl.multiple_of(r * rank, rank), rank), :]
            return (total + dot(lift[r], zeta_r)).astype(jnp.bfloat16)

        if final:
            each = owned // ncol
            first = [(c, i, lax.rem(mycol + c, ncol) * each + i) for c in range(1, ncol) for i in range(each)]
            for c, i, r in first:
                parts[step, r, mycol] = total_of(r)
                send(parts.at[step, r, mycol], parts.at[step, r, mycol],
                     part_s.at[step, i, c - 1], part_r.at[step, i, ncol - c - 1], 0, c)
            held = [mycol * each + i for i in range(each)]
            for r in held:
                parts[step, r, mycol] = total_of(r)
        else:
            held = list(range(owned))
            for r in held:
                parts[step, r, mycol] = total_of(r)
                for c in range(1, ncol):
                    send(parts.at[step, r, mycol], parts.at[step, r, mycol],
                         part_s.at[step, r, c - 1], part_r.at[step, r, ncol - c - 1], 0, c)
        count = step + 1
        sums = [0.0] * (2 * count + 1)
        for r in held:
            newest = current[r].astype(jnp.float32)
            for i in range(count):
                other = newest if i == step else member(i)[r].astype(jnp.float32)
                sums[count + 1 + i] += jnp.sum(newest * other, axis=0, keepdims=True)
        for i, r in enumerate(held):
            for c in range(1, ncol):
                arrived(parts.at[step, r, lax.rem(mycol + c, ncol)], part_r.at[step, i, c - 1])
            total = self_ref[r] * current[r].astype(jnp.float32)
            for k in range(ncol):
                total = total + parts[step, r, k].astype(jnp.float32)
            work[r] = total
            for i in range(count):
                sums[i] += jnp.sum(total * member(i)[r].astype(jnp.float32), axis=0, keepdims=True)
            sums[count] += jnp.sum(total * total, axis=0, keepdims=True)
        pad = [jnp.zeros((1, width), jnp.float32)] * (8 - len(sums))
        slot = me * ncol + mycol if final else me
        dots[step, slot] = jnp.concatenate(sums + pad, axis=0)
        peers = everyone if final else [(j, 0) for j in range(1, n)]
        for j, c in peers:
            send(dots.at[step, slot], dots.at[step, slot], dot_s.at[step, j, c],
                 dot_r.at[step, (n - j) % n, (ncol - c) % ncol], j, c)
        if not final:
            share_out(step + 1, work)
        for j, c in peers:
            theirs_at = lax.rem(me + j, n)
            if final:
                theirs_at = theirs_at * ncol + lax.rem(mycol + c, ncol)
            arrived(dots.at[step, theirs_at], dot_r.at[step, j, c])
        total = dots[step, 0]
        for k in range(1, n * ncol if final else n):
            total = total + dots[step, k]
        total = total / panels
        coefs = [total[i:i + 1] for i in range(count)]
        for i in range(count):
            gram[i, step] = gram[step, i] = total[count + 1 + i:count + 2 + i]
        square = total[count:count + 1]
        for i in range(count):
            inner = -2.0 * coefs[i]
            for k in range(count):
                inner = inner + coefs[k] * gram[i, k]
            square = square + coefs[i] * inner
        beta = jnp.sqrt(jnp.maximum(square, 0.0) + 1e-06)
        scale = 1.0 / beta
        for value in coefs + [beta]:
            hess_ref[line:line + 1, :] = value
            line += 1
        for i, r in enumerate(held):
            fresh = work[r]
            for k in range(count):
                fresh = fresh - coefs[k] * member(k)[r].astype(jnp.float32)
            fresh = (fresh * scale).astype(jnp.bfloat16)
            if final:
                last_ref[i * cls:(i + 1) * cls] = fresh
            else:
                basis[step, r] = fresh
    for copy in pending:
        copy.wait_send()


def on_device(vector, self_term, near_blocks, near_rows, near_source, send_index, source_basis,
              target_basis, couplings, far_rows, far_cols):
    owned, rank, cls = source_basis.shape
    width = vector.shape[1]
    n = lax.axis_size("blk")
    ncol = lax.axis_size("col")
    count, links = near_blocks.shape[0], couplings.shape[0]
    block = owned * rank
    piece = (cls + block) // ncol
    bf16, f32 = jnp.bfloat16, jnp.float32
    vmem, smem = pl.BlockSpec(memory_space=pltpu.VMEM), pl.BlockSpec(memory_space=pltpu.SMEM)
    hbm = pl.BlockSpec(memory_space=pl.ANY)
    dma = pltpu.SemaphoreType.DMA
    wide_self = jnp.broadcast_to(self_term.reshape(owned, cls, 1), (owned, cls, width))
    return pl.pallas_call(
        functools.partial(solve_kernel, n, ncol),
        out_shape=(
            jax.ShapeDtypeStruct((owned * cls // ncol, width), bf16),
            jax.ShapeDtypeStruct((ITERS * (ITERS + 3) // 2, width), f32),
        ),
        in_specs=[smem] * 5 + [hbm] + [vmem] * 5,
        out_specs=(vmem, vmem),
        scratch_shapes=[
            pltpu.VMEM((count + 1, cls, cls), bf16),
            pltpu.SMEM((count,), jnp.int32),
            pltpu.VMEM((rank, links, rank), f32),
            pltpu.VMEM((owned, cls, (owned + n - 1) * cls), bf16),
            pltpu.VMEM((block, links * rank), bf16),
            pltpu.VMEM((owned, cls, rank), bf16),
            pltpu.VMEM((ITERS - 1, owned, cls, width), bf16),
            pltpu.VMEM((owned, cls, width), f32),
            pltpu.VMEM((ITERS, n - 1, piece, width), bf16),
            pltpu.VMEM((ITERS, n - 1, ncol, piece, width), bf16),
            pltpu.VMEM((ITERS, n - 1, cls, width), bf16),
            pltpu.VMEM((n * block, width), bf16),
            pltpu.VMEM((ITERS, n * owned, rank, width), bf16),
            pltpu.VMEM((max(links * rank, block), width), bf16),
            pltpu.VMEM((ITERS, owned, ncol, cls, width), bf16),
            pltpu.VMEM((ITERS, n * ncol, 8, width), f32),
            dma,
            dma((ITERS, n - 1)), dma((ITERS, n - 1)),
            dma((ITERS, n - 1, ncol - 1)), dma((ITERS, n - 1, ncol - 1)),
            dma((ITERS, owned, ncol - 1)), dma((ITERS, owned, ncol - 1)),
            dma((ITERS, n, ncol)), dma((ITERS, n, ncol)),
        ],
        compiler_params=pltpu.CompilerParams(collective_id=0, has_side_effects=True, vmem_limit_bytes=59 << 20),
        name="solve",
    )(near_rows, near_source, send_index, far_rows, far_cols, near_blocks,
      vector.reshape(owned, cls, width), wide_self, source_basis, target_basis,
      couplings.transpose(1, 2, 0))


def solution(mesh):
    placed = (
        P(("grp", "blk"), "rhs"),
        P(("grp", "blk")),
        P(("grp", "blk", "col"), None, None),
        P(("grp", "blk", "col")),
        P(("grp", "blk", "col")),
        P(("grp", "blk"), None),
        P(("grp", "blk"), None, None),
        P(("grp", "blk"), None, None),
        P(("grp", "blk", "col"), None, None),
        P(("grp", "blk", "col")),
        P(("grp", "blk", "col")),
    )
    return jax.shard_map(
        on_device,
        mesh=mesh,
        in_specs=placed,
        out_specs=(P(("grp", "blk", "col"), "rhs"), P("grp", "rhs")),
        check_vma=False,
    )
```

time: 76.9 us -> 64.7 us (0.84)
  Pallas kernels: 69.2 us -> 59.2 us
  local copies, waits for them, and re-layouts: 6.04 us -> 4.55 us
    pallas_call x1 -> x0, Pallas kernels: 5.5 us -> none  [on_device(): pl.pallas_call(pack_kernel, out_shape=(jax.ShapeDtypeStruct((owned, cls,...]
    pallas_call x1, Pallas kernels: 63.7 us -> 59.2 us  [on_device(): pl.pallas_call(functools.partial(solve_kernel, n, ncol), out_shape=(jax.S...]
    unnamed x19 -> x2, local copies, waits for them, and re-layouts: 5.84 us -> 2.86 us
    broadcast_in_dim x2, local copies, waits for them, and re-layouts: 0.2 us -> 1.68 us  [on_device(): jnp.broadcast_to(self_term.reshape(owned, cls, 1), (owned, cls, width))]
where the time goes in v2:
time: 64.7 us; the launch traced here: 64.4 us
  Pallas kernels  59.2 us (91%)
  local copies, waits for them, and re-layouts  4.55 us (7%)
    pallas_call x1, Pallas kernels, on_device(): pl.pallas_call(functools.partial(solve_kernel, n, ncol), out_shape=(jax.S...  59.2 us
    unnamed x2, local copies, waits for them, and re-layouts  2.86 us
    broadcast_in_dim x2, local copies, waits for them, and re-layouts, on_device(): jnp.broadcast_to(self_term.reshape(owned, cls, 1), (owned, cls, width))  1.68 us

profile of v2, /device:TPU:0, one launch (start us, length us, event | category | flops | bytes accessed | tf_op | source)
XLA Modules:
  0.0 64.4 jit_solution(15731006023151361890)
XLA Ops:
  0.6 0.7 %broadcast_in_dim.7 = f32[4,256]{1,0:T(4,128)S(1)} reshape(f32[1024]{0:T(1024)} %param.12) | data formatting | bytes 8192 | tf_op jit(solution)/shard_map/broadcast_in_dim | solution.py:262
  1.3 1.0 %broadcast_in_dim.8.self_ref = f32[4,256,128]{2,1,0:T(8,128)} broadcast(f32[4,256]{1,0:T(4,128)S(1)} %broadcast_in_dim.7), dimensions={0,1} | broadcast | bytes 528384 | tf_op jit(solution)/shard_map/broadcast_in_dim | solution.py:262
  2.3 59.2 %solve.1 = (bf16[512,128]{1,0:T(8,128)(2,1)}, f32[9,128]{1,0:T(8,128)}) custom-call(s32[30]{0:T(128)} %rows.1, s32[30]{0:T(128)} %cols.1, s32[1,4]{1,0:T(1,128)} %send_ref.1, s32[64]{0:T(128)} %frows_ref.1, s32[64]{0:T(128)} %fcols_ref.1, bf16[30,256,256]{2,1,0:T(8,128)(2,1)} %near_in.1, bf16[4,256,128]{2,1,0:T(8,128)(2,1)} %bitcast.2, ...), custom_call_target="tpu_custom_call" | custom-call | tf_op jit(solution)/shard_map/solve/pallas_call | solution.py:263
  61.6 1.6 %copy.15 = bf16[512,128]{1,0:T(8,128)(2,1)} copy(bf16[512,128]{1,0:T(8,128)(2,1)} %get-tuple-element.4) | data formatting | bytes 262144
  63.1 1.3 %copy.16 = f32[9,128]{1,0:T(8,128)} copy(f32[9,128]{1,0:T(8,128)} %get-tuple-element.5) | data formatting | bytes 9216

commit v3 on v2

--- a/solution.py
+++ b/solution.py
@@ -15,7 +15,8 @@
     return jnp.dot(a, b, preferred_element_type=jnp.float32)
 
 
-def pack(n, rows, cols, near_in, coup_ref, frows_ref, target_ref, cells, keys, turned, dense, far, lift, near_sem):
+def pack(n, rows, cols, near_in, coup_ref, frows_ref, target_ref, self_ref, cells, keys, turned, dense, far, lift,
+         diagonal, near_sem, between):
     me = lax.axis_index("blk")
     count, cls, _ = near_in.shape
     owned = target_ref.shape[0]
@@ -52,6 +53,10 @@
             found = jnp.where(hit, b, found)
         return found
 
+    for i in range(self_ref.shape[0]):
+        column = jnp.broadcast_to(self_ref[i:i + 1], (diagonal.shape[1], 128)).T
+        diagonal[i * 128:(i + 1) * 128] = column
+    between()
     fetch.wait()
 
     @pl.loop(0, count)
@@ -67,16 +72,16 @@
 def solve_kernel(n, ncol, rows, cols, send_ref, frows_ref, fcols_ref, near_in, vector_ref, self_ref,
                  source_ref, target_ref, coup_ref,
                  last_ref, hess_ref,
-                 cells, keys, turned, dense, far, lift,
+                 cells, keys, turned, dense, far, lift, diagonal,
                  basis, work, outgoing, incoming, seg, raw, coef, chosen, parts, dots,
-                 near_sem, out_s, in_r, fwd_s, fwd_r, part_s, part_r, dot_s, dot_r):
+                 near_sem, out_s, in_r, fwd_s, fwd_r, coef_s, coef_r, part_s, part_r, dot_s, dot_r):
     me = lax.axis_index("blk")
     mycol = lax.axis_index("col")
     owned, cls, width = vector_ref.shape
     rank = source_ref.shape[1]
     panels = n * owned * cls
     block = owned * rank
-    share, cshare = cls // ncol, block // ncol
+    share = cls // ncol
     everyone = [(j, c) for j in range(n) for c in range(ncol) if j or c]
     barrier = pltpu.get_barrier_semaphore()
 
@@ -103,18 +108,17 @@
     def arrived(dst, rsem):
         pltpu.make_async_copy(dst, dst, rsem).wait()
 
-    def owner_rows(j):
-        return pl.multiple_of(lax.rem(me + j, n) * block, block)
-
-    def share_out(step, field):
-        for c in range(owned):
-            raw[pl.ds(owner_rows(0) + c * rank, rank), :] = dot(
-                source_ref[c], field[c].astype(jnp.bfloat16)).astype(jnp.bfloat16)
-        mine = raw[pl.ds(pl.multiple_of(owner_rows(0) + mycol * cshare, cshare), cshare), :]
+    def share_coef(step, c, field):
+        mine = raw.at[step, me * owned + c]
+        mine[...] = dot(source_ref[c], field.astype(jnp.bfloat16)).astype(jnp.bfloat16)
+        for j in range(1, n):
+            send(mine, mine, coef_s.at[step, c, j - 1], coef_r.at[step, c, n - j - 1], j, 0)
+
+    def share_segments(step, field):
         for j in range(1, n):
             pick = jnp.minimum(send_ref[0, lax.rem(me + j, n)], owned - 1)
-            outgoing[step, j - 1, :share] = field[pick, pl.ds(pl.multiple_of(mycol * share, share), share), :].astype(jnp.bfloat16)
-            outgoing[step, j - 1, share:] = mine
+            part = field[pick, pl.ds(pl.multiple_of(mycol * share, share), share), :]
+            outgoing[step, j - 1] = part.astype(jnp.bfloat16)
             send(outgoing.at[step, j - 1], incoming.at[step, n - j - 1, mycol],
                  out_s.at[step, j - 1], in_r.at[step, n - j - 1], j, 0)
 
@@ -129,43 +133,50 @@
         for j in range(1, n):
             for c in range(1, ncol):
                 arrived(incoming.at[step, j - 1, lax.rem(mycol + c, ncol)], fwd_r.at[step, j - 1, c - 1])
-            for k in range(ncol):
-                seg[step, j - 1, k * share:(k + 1) * share] = incoming[step, j - 1, k, :share]
-                raw[pl.ds(pl.multiple_of(owner_rows(j) + k * cshare, cshare), cshare), :] = incoming[step, j - 1, k, share:]
-
-    share_out(0, vector_ref)
-    pack(n, rows, cols, near_in, coup_ref, frows_ref, target_ref, cells, keys, turned, dense, far, lift, near_sem)
+
+    def collect_coefs(step):
+        for c in range(owned):
+            for j in range(1, n):
+                arrived(raw.at[step, lax.rem(me + j, n) * owned + c], coef_r.at[step, c, j - 1])
+
+    share_segments(0, vector_ref)
+    for c in range(owned):
+        share_coef(0, c, vector_ref[c])
+    pack(n, rows, cols, near_in, coup_ref, frows_ref, target_ref, self_ref, cells, keys, turned, dense, far, lift,
+         diagonal, near_sem, lambda: pass_on(0))
     coefs, scale = [], None
     for step in range(ITERS):
         current = member(step)
         final = step == ITERS - 1
-        pass_on(step)
         mine = current[...].reshape(owned * cls, width)
         for r in range(owned):
             work[r] = dot(dense[r, :, :owned * cls], mine)
-        collect(step)
-        if step == 0:
-            coef[0] = raw[...].reshape(n * owned, rank, width)
-        else:
-            fresh = raw[...].reshape(n * owned, rank, width).astype(jnp.float32)
+        collect_coefs(step)
+        fresh = raw[step]
+        if step:
+            fresh = fresh.astype(jnp.float32)
             for i in range(step):
                 fresh = fresh - coefs[i] * coef[i].astype(jnp.float32)
-            coef[step] = (fresh * scale).astype(jnp.bfloat16)
-            for j in range(n - 1):
-                fresh = seg[step, j].astype(jnp.float32)
-                for i in range(step):
-                    fresh = fresh - coefs[i] * seg[i, j].astype(jnp.float32)
-                seg[step, j] = (fresh * scale).astype(jnp.bfloat16)
+            fresh = (fresh * scale).astype(jnp.bfloat16)
+        coef[step] = fresh
         for f in range(fcols_ref.shape[0]):
             chosen[f * rank:(f + 1) * rank] = coef[step, fcols_ref[f]]
         zeta = dot(far[...], chosen[...]).astype(jnp.bfloat16)
-        chosen[:block] = zeta
+        for r in range(owned):
+            work[r] += dot(lift[r], zeta[r * rank:(r + 1) * rank])
+        collect(step)
+        for j in range(n - 1):
+            fresh = incoming[step, j].reshape(cls, width)
+            if step:
+                fresh = fresh.astype(jnp.float32)
+                for i in range(step):
+                    fresh = fresh - coefs[i] * seg[i, j].astype(jnp.float32)
+                fresh = (fresh * scale).astype(jnp.bfloat16)
+            seg[step, j] = fresh
         theirs = seg[step].reshape((n - 1) * cls, width)
 
         def total_of(r):
-            total = work[r] + dot(dense[r, :, owned * cls:], theirs)
-            zeta_r = chosen[pl.ds(pl.multiple_of(r * rank, rank), rank), :]
-            return (total + dot(lift[r], zeta_r)).astype(jnp.bfloat16)
+            return (work[r] + dot(dense[r, :, owned * cls:], theirs)).astype(jnp.bfloat16)
 
         if final:
             each = owned // ncol
@@ -194,10 +205,12 @@
         for i, r in enumerate(held):
             for c in range(1, ncol):
                 arrived(parts.at[step, r, lax.rem(mycol + c, ncol)], part_r.at[step, i, c - 1])
-            total = self_ref[r] * current[r].astype(jnp.float32)
+            total = diagonal[pl.ds(pl.multiple_of(r * cls, cls), cls), :] * current[r].astype(jnp.float32)
             for k in range(ncol):
                 total = total + parts[step, r, k].astype(jnp.float32)
             work[r] = total
+            if not final:
+                share_coef(step + 1, r, total)
             for i in range(count):
                 sums[i] += jnp.sum(total * member(i)[r].astype(jnp.float32), axis=0, keepdims=True)
             sums[count] += jnp.sum(total * total, axis=0, keepdims=True)
@@ -209,7 +222,7 @@
             send(dots.at[step, slot], dots.at[step, slot], dot_s.at[step, j, c],
                  dot_r.at[step, (n - j) % n, (ncol - c) % ncol], j, c)
         if not final:
-            share_out(step + 1, work)
+            share_segments(step + 1, work)
         for j, c in peers:
             theirs_at = lax.rem(me + j, n)
             if final:
@@ -230,6 +243,8 @@
             square = square + coefs[i] * inner
         beta = jnp.sqrt(jnp.maximum(square, 0.0) + 1e-06)
         scale = 1.0 / beta
+        if not final:
+            pass_on(step + 1)
         for value in coefs + [beta]:
             hess_ref[line:line + 1, :] = value
             line += 1
@@ -254,12 +269,11 @@
     ncol = lax.axis_size("col")
     count, links = near_blocks.shape[0], couplings.shape[0]
     block = owned * rank
-    piece = (cls + block) // ncol
+    share = cls // ncol
     bf16, f32 = jnp.bfloat16, jnp.float32
     vmem, smem = pl.BlockSpec(memory_space=pltpu.VMEM), pl.BlockSpec(memory_space=pltpu.SMEM)
     hbm = pl.BlockSpec(memory_space=pl.ANY)
     dma = pltpu.SemaphoreType.DMA
-    wide_self = jnp.broadcast_to(self_term.reshape(owned, cls, 1), (owned, cls, width))
     return pl.pallas_call(
         functools.partial(solve_kernel, n, ncol),
         out_shape=(
@@ -275,26 +289,28 @@
             pltpu.VMEM((owned, cls, (owned + n - 1) * cls), bf16),
             pltpu.VMEM((block, links * rank), bf16),
             pltpu.VMEM((owned, cls, rank), bf16),
+            pltpu.VMEM((owned * cls, width), f32),
             pltpu.VMEM((ITERS - 1, owned, cls, width), bf16),
             pltpu.VMEM((owned, cls, width), f32),
-            pltpu.VMEM((ITERS, n - 1, piece, width), bf16),
-            pltpu.VMEM((ITERS, n - 1, ncol, piece, width), bf16),
+            pltpu.VMEM((ITERS, n - 1, share, width), bf16),
+            pltpu.VMEM((ITERS, n - 1, ncol, share, width), bf16),
             pltpu.VMEM((ITERS, n - 1, cls, width), bf16),
-            pltpu.VMEM((n * block, width), bf16),
             pltpu.VMEM((ITERS, n * owned, rank, width), bf16),
-            pltpu.VMEM((max(links * rank, block), width), bf16),
+            pltpu.VMEM((ITERS, n * owned, rank, width), bf16),
+            pltpu.VMEM((links * rank, width), bf16),
             pltpu.VMEM((ITERS, owned, ncol, cls, width), bf16),
             pltpu.VMEM((ITERS, n * ncol, 8, width), f32),
             dma,
             dma((ITERS, n - 1)), dma((ITERS, n - 1)),
             dma((ITERS, n - 1, ncol - 1)), dma((ITERS, n - 1, ncol - 1)),
+            dma((ITERS, owned, n - 1)), dma((ITERS, owned, n - 1)),
             dma((ITERS, owned, ncol - 1)), dma((ITERS, owned, ncol - 1)),
             dma((ITERS, n, ncol)), dma((ITERS, n, ncol)),
         ],
         compiler_params=pltpu.CompilerParams(collective_id=0, has_side_effects=True, vmem_limit_bytes=59 << 20),
         name="solve",
     )(near_rows, near_source, send_index, far_rows, far_cols, near_blocks,
-      vector.reshape(owned, cls, width), wide_self, source_basis, target_basis,
+      vector.reshape(owned, cls, width), self_term.reshape(-1, 128), source_basis, target_basis,
       couplings.transpose(1, 2, 0))
 
 

time: 64.7 us -> 60.2 us (0.930)
  Pallas kernels: 59.2 us -> 56.5 us
  local copies, waits for them, and re-layouts: 4.55 us -> 2.86 us
    pallas_call x1, Pallas kernels: 59.2 us -> 56.5 us  [on_device(): pl.pallas_call(functools.partial(solve_kernel, n, ncol), out_shape=(jax.S...]
    broadcast_in_dim x2 -> x0, local copies, waits for them, and re-layouts: 1.68 us -> none  [on_device(): jnp.broadcast_to(self_term.reshape(owned, cls, 1), (owned, cls, width))]
where the time goes in v3:
time: 60.2 us; the launch traced here: 60 us
  Pallas kernels  56.5 us (94%)
  local copies, waits for them, and re-layouts  2.86 us (5%)
  between operations  0.64 us (1%)
    pallas_call x1, Pallas kernels, on_device(): pl.pallas_call(functools.partial(solve_kernel, n, ncol), out_shape=(jax.S...  56.5 us
    unnamed x2, local copies, waits for them, and re-layouts  2.86 us

profile of v3, /device:TPU:0, one launch (start us, length us, event | category | flops | bytes accessed | tf_op | source)
XLA Modules:
  0.0 60.0 jit_solution(14634970819606088612)
XLA Ops:
  0.6 56.5 %solve.1 = (bf16[512,128]{1,0:T(8,128)(2,1)}, f32[9,128]{1,0:T(8,128)}) custom-call(s32[30]{0:T(128)} %rows.1, s32[30]{0:T(128)} %cols.1, s32[1,4]{1,0:T(1,128)} %send_ref.1, s32[64]{0:T(128)} %frows_ref.1, s32[64]{0:T(128)} %fcols_ref.1, bf16[30,256,256]{2,1,0:T(8,128)(2,1)} %near_in.1, bf16[4,256,128]{2,1,0:T(8,128)(2,1)} %bitcast.3, f32[8,128]{1,0:T(8,128)} %bitcast.5, ...), custom_call_target="tpu_custom_call" | custom-call | tf_op jit(solution)/shard_map/solve/pallas_call | solution.py:277
  57.2 1.6 %copy.15 = bf16[512,128]{1,0:T(8,128)(2,1)} copy(bf16[512,128]{1,0:T(8,128)(2,1)} %get-tuple-element.4) | data formatting | bytes 262144
  58.7 1.3 %copy.16 = f32[9,128]{1,0:T(8,128)} copy(f32[9,128]{1,0:T(8,128)} %get-tuple-element.5) | data formatting | bytes 9216

commit v4 on v3

--- a/solution.py
+++ b/solution.py
@@ -117,9 +117,14 @@
     def share_segments(step, field):
         for j in range(1, n):
             pick = jnp.minimum(send_ref[0, lax.rem(me + j, n)], owned - 1)
+            if step:
+                outgoing[step, j - 1] = field[pick].astype(jnp.bfloat16).reshape(ncol, share, width)
+                send(outgoing.at[step, j - 1], incoming.at[step, n - j - 1],
+                     out_s.at[step, j - 1], in_r.at[step, n - j - 1], j, 0)
+                continue
             part = field[pick, pl.ds(pl.multiple_of(mycol * share, share), share), :]
-            outgoing[step, j - 1] = part.astype(jnp.bfloat16)
-            send(outgoing.at[step, j - 1], incoming.at[step, n - j - 1, mycol],
+            outgoing[step, j - 1, 0] = part.astype(jnp.bfloat16)
+            send(outgoing.at[step, j - 1, 0], incoming.at[step, n - j - 1, mycol],
                  out_s.at[step, j - 1], in_r.at[step, n - j - 1], j, 0)
 
     def pass_on(step):
@@ -131,6 +136,9 @@
 
     def collect(step):
         for j in range(1, n):
+            if step:
+                arrived(incoming.at[step, j - 1], in_r.at[step, j - 1])
+                continue
             for c in range(1, ncol):
                 arrived(incoming.at[step, j - 1, lax.rem(mycol + c, ncol)], fwd_r.at[step, j - 1, c - 1])
 
@@ -243,8 +251,6 @@
             square = square + coefs[i] * inner
         beta = jnp.sqrt(jnp.maximum(square, 0.0) + 1e-06)
         scale = 1.0 / beta
-        if not final:
-            pass_on(step + 1)
         for value in coefs + [beta]:
             hess_ref[line:line + 1, :] = value
             line += 1
@@ -272,7 +278,7 @@
     share = cls // ncol
     bf16, f32 = jnp.bfloat16, jnp.float32
     vmem, smem = pl.BlockSpec(memory_space=pltpu.VMEM), pl.BlockSpec(memory_space=pltpu.SMEM)
-    hbm = pl.BlockSpec(memory_space=pl.ANY)
+    hbm = pl.BlockSpec(memory_space=pltpu.HBM)
     dma = pltpu.SemaphoreType.DMA
     return pl.pallas_call(
         functools.partial(solve_kernel, n, ncol),
@@ -292,7 +298,7 @@
             pltpu.VMEM((owned * cls, width), f32),
             pltpu.VMEM((ITERS - 1, owned, cls, width), bf16),
             pltpu.VMEM((owned, cls, width), f32),
-            pltpu.VMEM((ITERS, n - 1, share, width), bf16),
+            pltpu.VMEM((ITERS, n - 1, ncol, share, width), bf16),
             pltpu.VMEM((ITERS, n - 1, ncol, share, width), bf16),
             pltpu.VMEM((ITERS, n - 1, cls, width), bf16),
             pltpu.VMEM((ITERS, n * owned, rank, width), bf16),
@@ -307,7 +313,7 @@
             dma((ITERS, owned, ncol - 1)), dma((ITERS, owned, ncol - 1)),
             dma((ITERS, n, ncol)), dma((ITERS, n, ncol)),
         ],
-        compiler_params=pltpu.CompilerParams(collective_id=0, has_side_effects=True, vmem_limit_bytes=59 << 20),
+        compiler_params=pltpu.CompilerParams(collective_id=0, has_side_effects=True, vmem_limit_bytes=60 << 20),
         name="solve",
     )(near_rows, near_source, send_index, far_rows, far_cols, near_blocks,
       vector.reshape(owned, cls, width), self_term.reshape(-1, 128), source_basis, target_basis,

time: 60.2 us -> 56.8 us (0.944)
  Pallas kernels: 56.5 us -> 53.1 us
    pallas_call x1, Pallas kernels: 56.5 us -> 53.1 us  [on_device(): pl.pallas_call(functools.partial(solve_kernel, n, ncol), out_shape=(jax.S...]
where the time goes in v4:
time: 56.8 us; the launch traced here: 56.6 us
  Pallas kernels  53.1 us (93%)
  local copies, waits for them, and re-layouts  2.86 us (5%)
  between operations  0.64 us (1%)
    pallas_call x1, Pallas kernels, on_device(): pl.pallas_call(functools.partial(solve_kernel, n, ncol), out_shape=(jax.S...  53.1 us
    unnamed x2, local copies, waits for them, and re-layouts  2.86 us

profile of v4, /device:TPU:0, one launch (start us, length us, event | category | flops | bytes accessed | tf_op | source)
XLA Modules:
  0.0 56.6 jit_solution(16813771974463251517)
XLA Ops:
  0.6 53.1 %solve.1 = (bf16[512,128]{1,0:T(8,128)(2,1)}, f32[9,128]{1,0:T(8,128)}) custom-call(s32[30]{0:T(128)} %rows.1, s32[30]{0:T(128)} %cols.1, s32[1,4]{1,0:T(1,128)} %send_ref.1, s32[64]{0:T(128)} %frows_ref.1, s32[64]{0:T(128)} %fcols_ref.1, bf16[30,256,256]{2,1,0:T(8,128)(2,1)} %near_in.1, bf16[4,256,128]{2,1,0:T(8,128)(2,1)} %bitcast.3, f32[8,128]{1,0:T(8,128)} %bitcast.5, ...), custom_call_target="tpu_custom_call" | custom-call | tf_op jit(solution)/shard_map/solve/pallas_call | solution.py:283
  53.7 1.6 %copy.15 = bf16[512,128]{1,0:T(8,128)(2,1)} copy(bf16[512,128]{1,0:T(8,128)(2,1)} %get-tuple-element.4) | data formatting | bytes 262144
  55.3 1.3 %copy.16 = f32[9,128]{1,0:T(8,128)} copy(f32[9,128]{1,0:T(8,128)} %get-tuple-element.5) | data formatting | bytes 9216
